TPU v7x, 32 devices: a whole 2x2x4 slice. The times are simulated.
32 devices in a mesh: row: 4 (over x, core), col: 4 (over z), layer: 2 (over y).
Axes of the slice: x: 2, y: 2, z: 4, core: 2. Of those that a mesh axis runs over, the one named last changes fastest.
Arguments:
- amplitudes: float32 [1536, 16384], P(('row', 'col', 'layer')), may hold values from -6 to 6
- integrals: float32 [16384, 2048], P(('col', 'layer')), may hold values from -0.046875 to 0.046875
- pair_list: int32 [1536, 2], P(('row', 'col', 'layer')), may hold values from 0 to 199, as said below
- occupied_energy: float32 [200], replicated, may hold values from -1.5 to -0.3
- virtual_energy: float32 [2048], replicated, may hold values from 1 to 4
Outputs:
- ladder_update: float32 [1536, 2048], P(('row', 'col', 'layer'))
Inputs may be any that keep to these rules, and one draw needn't show every extreme that they name: `pair_list`: each row (i, j) holds two occupied orbital numbers with i <= j.
All inputs are finite; a program needn't handle non-finite values.
Results may differ from a plain program's by a relative error of at most 0.000071.
Values sent between devices are 32-bit elements; how exact they have to be, the bound alone decides.
A program may use at most 128 MiB of HBM per device.

v0:
```python
import jax
import jax.numpy as jnp
from jax import lax
from jax.sharding import PartitionSpec as P


def energy_lookup(pair_list, occupied_energy):
    occ_index = jnp.arange(occupied_energy.shape[0], dtype=jnp.int32)
    occ_first = jnp.sum(
        jnp.where(pair_list[:, 0:1] == occ_index[None, :], occupied_energy[None, :], 0.0), axis=1
    )
    occ_second = jnp.sum(
        jnp.where(pair_list[:, 1:2] == occ_index[None, :], occupied_energy[None, :], 0.0), axis=1
    )
    return (occ_first, occ_second)


def body(amplitudes, integrals, pair_list, occupied_energy, virtual_energy):
    row_count = amplitudes.shape[0]
    group_count = lax.axis_size(("col", "layer"))
    shaped = amplitudes.reshape(row_count, group_count, amplitudes.shape[1] // group_count)
    partial_value = jnp.einsum(
        "rsk,kn->rsn",
        lax.all_to_all(shaped, ("col", "layer"), split_axis=1, concat_axis=1, tiled=True),
        integrals,
        precision=lax.Precision.HIGHEST,
        preferred_element_type=jnp.float32,
    )
    returned = lax.all_to_all(
        partial_value, ("col", "layer"), split_axis=1, concat_axis=1, tiled=True
    )
    ladder = jnp.sum(returned, axis=1)
    occ_first, occ_second = energy_lookup(pair_list, occupied_energy)
    denominator = virtual_energy[None, :] - occ_first[:, None] - occ_second[:, None]
    return ladder / denominator


def solution(mesh):
    in_specs = (
        P(("row", "col", "layer"), None),
        P(("col", "layer"), None),
        P(("row", "col", "layer"), None),
        P(),
        P(),
    )
    out_specs = P(("row", "col", "layer"), None)
    return jax.shard_map(body, mesh=mesh, in_specs=in_specs, out_specs=out_specs, check_vma=False)
```

profile of v0, /device:TPU:0, one launch (start us, length us, event | category | flops | bytes accessed | tf_op | source)
XLA Modules:
  0.0 179.3 jit_solution(14689147398900079940)
XLA Ops:
  0.0 2.1 %copy.18 = f32[6,8,8,2048]{3,2,0,1:T(8,128)S(1)} copy(f32[6,8,8,2048]{3,2,1,0:T(8,128)} %bitcast.13) | data formatting | bytes 6291456 | tf_op jit(solution)/shard_map/reshape | solution.py:21
  2.1 77.8 %all_to_all.10 = f32[48,8,2048]{2,0,1:T(8,128)S(1)} all-to-all(f32[48,8,2048]{2,0,1:T(8,128)S(1)} %bitcast.12), channel_id=1, replica_groups=mesh['row'=4,'col'=4,'layer'=2] {'col','layer'}, dimensions={1} | all-to-all | bytes 6291456 | tf_op jit(solution)/shard_map/all_to_all | solution.py:24
  79.9 24.2 %fusion = f32[48,8,2048]{2,0,1:T(8,128)} fusion(f32[48,8,2048]{2,0,1:T(8,128)S(1)} %all_to_all.10, f32[2048,2048]{1,0:T(8,128)} %param.6), kind=kOutput, calls=%fused_computation | convolution fusion | flops 19327352832 | bytes 23068672 | tf_op jit(solution)/shard_map/rsk,kn->rsn/dot_general | solution.py:22
  104.1 0.0 copy-start.2
  104.1 0.0 copy-start.1
  104.1 3.8 %all-to-all-start.1 = ((f32[48,8,2048]{2,0,1:T(8,128)}), f32[48,8,2048]{2,0,1:T(8,128)S(1)}, u32[]{:S(2)}, u32[]{:S(2)}) async-start(f32[48,8,2048]{2,0,1:T(8,128)} %fusion), calls=%async_computation.1 | async-start | bytes 6291456 | tf_op jit(solution)/shard_map/all_to_all | solution.py:29
  107.9 0.0 copy-done.2
  107.9 0.0 copy-start
  107.9 0.0 copy-done.1
  107.9 0.2 select_reduce_fusion.1
  108.1 70.1 %all-to-all-done.1 = f32[48,8,2048]{2,0,1:T(8,128)S(1)} async-done(((f32[48,8,2048]{2,0,1:T(8,128)}), f32[48,8,2048]{2,0,1:T(8,128)S(1)}, u32[]{:S(2)}, u32[]{:S(2)}) %all-to-all-start.1) | async-done | bytes 3145760 | tf_op jit(solution)/shard_map/all_to_all | solution.py:29
  178.2 0.2 reduce_sum.27
  178.4 0.0 copy-done
  178.4 0.9 subtract_divide_fusion
  (1 shorter events, 0.0 us)
Async XLA Ops:
  104.1 3.8 %copy-start.2 = (s32[48,2]{0,1:T(2,128)S(1)}, s32[48,2]{0,1:T(2,128)}, u32[]{:S(2)}) copy-start(s32[48,2]{0,1:T(2,128)} %param.7) | copy-start | bytes 1156
  104.1 3.8 %copy-start.1 = (f32[200]{0:T(256)S(1)}, f32[200]{0:T(256)}, u32[]{:S(2)}) copy-start(f32[200]{0:T(256)} %param.8) | copy-start | bytes 2404
  104.1 74.1 %all-to-all-start.1 = ((f32[48,8,2048]{2,0,1:T(8,128)}), f32[48,8,2048]{2,0,1:T(8,128)S(1)}, u32[]{:S(2)}, u32[]{:S(2)}) async-start(f32[48,8,2048]{2,0,1:T(8,128)} %fusion), calls=%async_computation.1 | async-start | bytes 6291456 | tf_op jit(solution)/shard_map/all_to_all | solution.py:29
  107.9 70.5 %copy-start = (f32[2048]{0:T(1024)S(1)}, f32[2048]{0:T(1024)}, u32[]{:S(2)}) copy-start(f32[2048]{0:T(1024)} %param.9) | copy-start | bytes 24580
where the time goes:
time: 180 us; the launch traced here: 179 us
  blocking collectives  77.8 us (43%)
  waiting for transfers between devices  70.1 us (39%)
  matrix products  24.2 us (13%)
  starting transfers between devices  3.78 us (2%)
  local copies, waits for them, and re-layouts  2.11 us (1%)
    all_to_all x1, blocking collectives, body(): lax.all_to_all(shaped, ('col', 'layer'), split_axis=1, concat_axis=1, til...  77.8 us
    all_to_all x1, waiting for transfers between devices, body(): lax.all_to_all(partial_value, ('col', 'layer'), split_axis=1, concat_axis...  70.1 us
    dot_general x1, matrix products, body(): jnp.einsum('rsk,kn->rsn', lax.all_to_all(shaped, ('col', 'layer'), split_...  24.2 us
    all_to_all x1, starting transfers between devices, body(): lax.all_to_all(partial_value, ('col', 'layer'), split_axis=1, concat_axis...  3.78 us
  transfers between devices with their start and end apart: 1, of which 1 were waited for; matrix products, arithmetic and copies ran while one was open for 0% of the time, Pallas kernels for 0%

commit v1 on v0

v1 whole, which is shorter than its diff:
```python
import functools

import jax
import jax.numpy as jnp
from jax import lax
from jax.experimental import pallas as pl
from jax.experimental.pallas import tpu as pltpu
from jax.sharding import PartitionSpec as P

MESH = pl.DeviceIdType.MESH
CHUNKS = (24, 16, 8)
TILE = 512
AHEAD = 1


def reverse_bits(value, bits):
    out = 0
    for bit in range(bits):
        out |= ((value >> bit) & 1) << (bits - 1 - bit)
    return out


def peer_id(me, k, layers):
    other = jnp.bitwise_xor(me, k)
    return {"col": other // layers, "layer": lax.rem(other, layers)}


def kernel(
    group, layers, chunks, amp, ints, out, got, part, back, high, low, amp_high, amp_low, stage,
    stage_sem, own_sem, amp_send, amp_recv, back_send, back_recv,
):
    bits = group.bit_length() - 1
    depth = ints.shape[0]
    columns = ints.shape[1]
    tiles = columns // TILE
    me = lax.axis_index("col") * layers + lax.axis_index("layer")

    barrier = pltpu.get_barrier_semaphore()
    for k in range(1, group):
        pl.semaphore_signal(barrier, inc=1, device_id=peer_id(me, k, layers), device_id_type=MESH)

    def load_tile(t, slot):
        cols = pl.ds(pl.multiple_of(t * TILE, TILE), TILE)
        return pltpu.make_async_copy(ints.at[:, cols], stage.at[slot], stage_sem.at[slot])

    load_tile(0, 0).start()

    starts = [sum(chunks[:c]) for c in range(len(chunks))]

    def ef_columns(k):
        return pl.ds(pl.multiple_of(jnp.bitwise_xor(me, k) * depth, depth), depth)

    def amp_copy(c, k):
        slot = reverse_bits(k, bits)
        rows = pl.ds(starts[c], chunks[c])
        return pltpu.make_async_remote_copy(
            src_ref=amp.at[rows, ef_columns(k)],
            dst_ref=got.at[slot, rows, :],
            send_sem=amp_send.at[c, slot],
            recv_sem=amp_recv.at[c, slot],
            device_id=peer_id(me, k, layers),
            device_id_type=MESH,
        )

    def send_amp(c):
        for k in reversed(range(1, group)):
            amp_copy(c, k).start()

    own = pltpu.make_async_copy(amp.at[:, ef_columns(0)], got.at[0], own_sem)

    pl.semaphore_wait(barrier, group - 1)
    for c in range(min(AHEAD, len(chunks))):
        send_amp(c)
    own.start()

    @pl.loop(0, tiles)
    def _(t):
        slot = lax.rem(t, 2)

        @pl.when(t + 1 < tiles)
        def _():
            load_tile(t + 1, 1 - slot).start()

        load_tile(t, slot).wait()
        cols = pl.ds(pl.multiple_of(t * TILE, TILE), TILE)
        step = min(depth, 256)

        @pl.loop(0, depth // step)
        def _(i):
            rows = pl.ds(pl.multiple_of(i * step, step), step)
            value = stage[slot, rows, :]
            top = value.astype(jnp.bfloat16)
            high[rows, cols] = top
            low[rows, cols] = (value - top.astype(jnp.float32)).astype(jnp.bfloat16)

    own.wait()

    def back_copy(c, s, t):
        half = group >> (s + 1)
        rows = pl.ds(starts[c], chunks[c])
        cols = pl.ds(pl.multiple_of(t * TILE, TILE), TILE)
        return pltpu.make_async_remote_copy(
            src_ref=part.at[pl.ds(half, half), rows, cols],
            dst_ref=back.at[pl.ds(group - 2 * half, half), rows, cols],
            send_sem=back_send.at[c, s, t],
            recv_sem=back_recv.at[c, s, t],
            device_id=peer_id(me, 1 << s, layers),
            device_id_type=MESH,
        )

    def add_back(c, s, t):
        half = group >> (s + 1)
        rows = pl.ds(starts[c], chunks[c])
        cols = pl.ds(pl.multiple_of(t * TILE, TILE), TILE)
        back_copy(c, s, t).wait_recv()
        if s == bits - 1:
            out[rows, cols] = part[0, rows, cols] + back[group - 2, rows, cols]
            return
        kept = pl.ds(0, half)
        part[kept, rows, cols] += back[pl.ds(group - 2 * half, half), rows, cols]
        back_copy(c, s + 1, t).start()

    def compute(c):
        count = group * chunks[c]
        rows = pl.ds(starts[c], chunks[c])

        @pl.loop(0, tiles)
        def _(t):
            cols = pl.ds(pl.multiple_of(t * TILE, TILE), TILE)
            both = jnp.dot(amp_high[pl.ds(0, count), :], high[:, cols], preferred_element_type=jnp.float32)
            both += jnp.dot(amp_high[pl.ds(0, count), :], low[:, cols], preferred_element_type=jnp.float32)
            both += jnp.dot(amp_low[pl.ds(0, count), :], high[:, cols], preferred_element_type=jnp.float32)
            part[:, rows, cols] = both.reshape(group, chunks[c], TILE)
            back_copy(c, 0, t).start()

    last = len(chunks) - 1
    for c in range(len(chunks)):
        for k in reversed(range(1, group)):
            amp_copy(c, k).wait_recv()
        if c + AHEAD <= last:
            send_amp(c + AHEAD)
        rows = pl.ds(starts[c], chunks[c])
        value = got[:, rows, :].reshape(group * chunks[c], depth)
        top = value.astype(jnp.bfloat16)
        amp_high[pl.ds(0, group * chunks[c]), :] = top
        amp_low[pl.ds(0, group * chunks[c]), :] = (value - top.astype(jnp.float32)).astype(jnp.bfloat16)
        compute(c)
        if c > 0:
            for t in range(tiles):
                add_back(c - 1, bits - 1, t)
        stop = bits if c == last else bits - 1
        for i in range(tiles + stop - 1):
            for s in range(stop):
                if 0 <= i - s < tiles:
                    add_back(c, s, i - s)

    for c in range(len(chunks)):
        for k in range(1, group):
            amp_copy(c, k).wait_send()
        for s in range(bits):
            for t in range(tiles):
                back_copy(c, s, t).wait_send()


def energy_lookup(pair_list, occupied_energy):
    occ_index = jnp.arange(occupied_energy.shape[0], dtype=jnp.int32)
    occ_first = jnp.sum(
        jnp.where(pair_list[:, 0:1] == occ_index[None, :], occupied_energy[None, :], 0.0), axis=1
    )
    occ_second = jnp.sum(
        jnp.where(pair_list[:, 1:2] == occ_index[None, :], occupied_energy[None, :], 0.0), axis=1
    )
    return (occ_first, occ_second)


def body(group, layers, amplitudes, integrals, pair_list, occupied_energy, virtual_energy):
    count = amplitudes.shape[0]
    depth, columns = integrals.shape
    bits = group.bit_length() - 1
    tiles = columns // TILE
    chunks = CHUNKS
    most = group * max(chunks)
    n = len(chunks)
    ladder = pl.pallas_call(
        functools.partial(kernel, group, layers, chunks),
        out_shape=jax.ShapeDtypeStruct((count, columns), jnp.float32),
        in_specs=[pl.BlockSpec(memory_space=pl.ANY)] * 2,
        out_specs=pl.BlockSpec(memory_space=pltpu.VMEM),
        scratch_shapes=[
            pltpu.VMEM((group, count, depth), jnp.float32),
            pltpu.VMEM((group, count, columns), jnp.float32),
            pltpu.VMEM((group - 1, count, columns), jnp.float32),
            pltpu.VMEM((depth, columns), jnp.bfloat16),
            pltpu.VMEM((depth, columns), jnp.bfloat16),
            pltpu.VMEM((most, depth), jnp.bfloat16),
            pltpu.VMEM((most, depth), jnp.bfloat16),
            pltpu.VMEM((2, depth, TILE), jnp.float32),
            pltpu.SemaphoreType.DMA((2,)),
            pltpu.SemaphoreType.DMA,
            pltpu.SemaphoreType.DMA((n, group)),
            pltpu.SemaphoreType.DMA((n, group)),
            pltpu.SemaphoreType.DMA((n, bits, tiles)),
            pltpu.SemaphoreType.DMA((n, bits, tiles)),
        ],
        compiler_params=pltpu.CompilerParams(
            collective_id=0, has_side_effects=True, vmem_limit_bytes=63 * 1024 * 1024
        ),
        cost_estimate=pl.CostEstimate(
            flops=6 * group * count * depth * columns, bytes_accessed=4 * (count * group * depth + depth * columns),
            transcendentals=0,
        ),
    )(amplitudes, integrals)
    occ_first, occ_second = energy_lookup(pair_list, occupied_energy)
    denominator = virtual_energy[None, :] - occ_first[:, None] - occ_second[:, None]
    return ladder / denominator


def solution(mesh):
    in_specs = (
        P(("row", "col", "layer"), None),
        P(("col", "layer"), None),
        P(("row", "col", "layer"), None),
        P(),
        P(),
    )
    out_specs = P(("row", "col", "layer"), None)
    layers = mesh.shape["layer"]
    group = mesh.shape["col"] * layers
    return jax.shard_map(
        functools.partial(body, group, layers), mesh=mesh, in_specs=in_specs, out_specs=out_specs, check_vma=False
    )
```

time: 180 us -> 120 us (0.67)
  Pallas kernels: 0 us -> 116 us
  blocking collectives: 77.8 us -> 0 us
  waiting for transfers between devices: 70.1 us -> 0 us
  matrix products: 24.2 us -> 0 us
  starting transfers between devices: 3.78 us -> 0 us
    pallas_call x0 -> x1, Pallas kernels: none -> 116 us  [body(): pl.pallas_call(functools.partial(kernel, group, layers, chunks), out_shap...]
    all_to_all x1 -> x0, blocking collectives: 77.8 us -> none  [body(): lax.all_to_all(shaped, ('col', 'layer'), split_axis=1, concat_axis=1, til...]
    all_to_all x1 -> x0, waiting for transfers between devices: 70.1 us -> none  [body(): lax.all_to_all(partial_value, ('col', 'layer'), split_axis=1, concat_axis...]
    dot_general x1 -> x0, matrix products: 24.2 us -> none  [body(): jnp.einsum('rsk,kn->rsn', lax.all_to_all(shaped, ('col', 'layer'), split_...]
    all_to_all x1 -> x0, starting transfers between devices: 3.78 us -> none  [body(): lax.all_to_all(partial_value, ('col', 'layer'), split_axis=1, concat_axis...]
    reshape x1 -> x0, local copies, waits for them, and re-layouts: 2.09 us -> none  [body(): amplitudes.reshape(row_count, group_count, amplitudes.shape[1] // group_c...]
  transfers between devices with their start and end apart: 1 -> 0, of which waited for: 1 -> 0; matrix products, arithmetic and copies ran while one was open for 0% -> 0% of each run, Pallas kernels for 0% -> 0%
where the time goes in v1:
time: 120 us
  Pallas kernels  116 us (97%)
  other arithmetic  2.74 us (2%)
    pallas_call x1, Pallas kernels, body(): pl.pallas_call(functools.partial(kernel, group, layers, chunks), out_shap...  116 us

profile of v1, /device:TPU:0, one launch (start us, length us, event | category | flops | bytes accessed | tf_op | source)
XLA Modules:
  0.0 119.9 jit_solution(3538575212426137923)
XLA Ops:
  0.0 0.8 slice_bitcast_fusion
  0.8 0.9 select_reduce_fusion.1
  1.6 0.0 copy-start
  1.6 116.3 %shard_map.55 = f32[48,2048]{1,0:T(8,128)} custom-call(f32[48,16384]{1,0:T(8,128)} %amp.1, f32[2048,2048]{1,0:T(8,128)} %ints.1), custom_call_target="tpu_custom_call" | custom-call | flops 9663676416 | bytes 19922944 | tf_op jit(solution)/shard_map/pallas_call | solution.py:184
  118.0 0.0 copy-done
  118.0 1.9 %subtract_divide_fusion = f32[48,2048]{1,0:T(8,128)} fusion(f32[48,2048]{1,0:T(8,128)} %shard_map.55, f32[48]{0:T(128)S(1)} %get-tuple-element.6, f32[48]{0:T(128)S(1)} %get-tuple-element.5, f32[2048]{0:T(1024)S(1)} %copy-done), kind=kLoop, calls=%fused_computation | loop fusion | flops 294912 | bytes 795008 | tf_op jit(solution)/shard_map/div | solution.py:215
Async XLA Ops:
  1.6 116.3 %copy-start = (f32[2048]{0:T(1024)S(1)}, f32[2048]{0:T(1024)}, u32[]{:S(2)}) copy-start(f32[2048]{0:T(1024)} %param.9) | copy-start | bytes 24580

commit v2 on v1

--- a/solution.py
+++ b/solution.py
@@ -8,9 +8,11 @@
 from jax.sharding import PartitionSpec as P
 
 MESH = pl.DeviceIdType.MESH
-CHUNKS = (24, 16, 8)
+CHUNKS = (16, 16, 16)
 TILE = 512
-AHEAD = 1
+RETURN = 1024
+LAST = 512
+AHEAD = 2
 
 
 def reverse_bits(value, bits):
@@ -95,10 +97,21 @@
 
     own.wait()
 
+    last = len(chunks) - 1
+
+    def width(c):
+        return LAST if c == last else RETURN
+
+    def tiles_of(c):
+        return columns // width(c)
+
+    def tile_columns(c, t):
+        return pl.ds(pl.multiple_of(t * width(c), width(c)), width(c))
+
     def back_copy(c, s, t):
         half = group >> (s + 1)
         rows = pl.ds(starts[c], chunks[c])
-        cols = pl.ds(pl.multiple_of(t * TILE, TILE), TILE)
+        cols = tile_columns(c, t)
         return pltpu.make_async_remote_copy(
             src_ref=part.at[pl.ds(half, half), rows, cols],
             dst_ref=back.at[pl.ds(group - 2 * half, half), rows, cols],
@@ -111,7 +124,7 @@
     def add_back(c, s, t):
         half = group >> (s + 1)
         rows = pl.ds(starts[c], chunks[c])
-        cols = pl.ds(pl.multiple_of(t * TILE, TILE), TILE)
+        cols = tile_columns(c, t)
         back_copy(c, s, t).wait_recv()
         if s == bits - 1:
             out[rows, cols] = part[0, rows, cols] + back[group - 2, rows, cols]
@@ -120,45 +133,56 @@
         part[kept, rows, cols] += back[pl.ds(group - 2 * half, half), rows, cols]
         back_copy(c, s + 1, t).start()
 
+    def add_all(c, s):
+        for t in range(tiles_of(c)):
+            add_back(c, s, t)
+
     def compute(c):
         count = group * chunks[c]
         rows = pl.ds(starts[c], chunks[c])
-
-        @pl.loop(0, tiles)
+        value = got[:, rows, :].reshape(count, depth)
+        top = value.astype(jnp.bfloat16)
+        amp_high[pl.ds(0, count), :] = top
+        amp_low[pl.ds(0, count), :] = (value - top.astype(jnp.float32)).astype(jnp.bfloat16)
+
+        @pl.loop(0, tiles_of(c))
         def _(t):
-            cols = pl.ds(pl.multiple_of(t * TILE, TILE), TILE)
+            cols = tile_columns(c, t)
             both = jnp.dot(amp_high[pl.ds(0, count), :], high[:, cols], preferred_element_type=jnp.float32)
             both += jnp.dot(amp_high[pl.ds(0, count), :], low[:, cols], preferred_element_type=jnp.float32)
             both += jnp.dot(amp_low[pl.ds(0, count), :], high[:, cols], preferred_element_type=jnp.float32)
-            part[:, rows, cols] = both.reshape(group, chunks[c], TILE)
+            part[:, rows, cols] = both.reshape(group, chunks[c], width(c))
             back_copy(c, 0, t).start()
 
-    last = len(chunks) - 1
     for c in range(len(chunks)):
         for k in reversed(range(1, group)):
             amp_copy(c, k).wait_recv()
         if c + AHEAD <= last:
             send_amp(c + AHEAD)
-        rows = pl.ds(starts[c], chunks[c])
-        value = got[:, rows, :].reshape(group * chunks[c], depth)
-        top = value.astype(jnp.bfloat16)
-        amp_high[pl.ds(0, group * chunks[c]), :] = top
-        amp_low[pl.ds(0, group * chunks[c]), :] = (value - top.astype(jnp.float32)).astype(jnp.bfloat16)
         compute(c)
-        if c > 0:
-            for t in range(tiles):
-                add_back(c - 1, bits - 1, t)
-        stop = bits if c == last else bits - 1
-        for i in range(tiles + stop - 1):
-            for s in range(stop):
-                if 0 <= i - s < tiles:
-                    add_back(c, s, i - s)
+        for s in range(1, bits):
+            if c - s >= 0:
+                add_all(c - s, s)
+        if c < last:
+            add_all(c, 0)
+
+    left = [(c, s) for c in range(last) for s in range(last - c + 1, bits)]
+    for c, s in left:
+        if s < bits - 1:
+            add_all(c, s)
+    for i in range(tiles_of(last) + bits - 1):
+        for s in range(bits):
+            if 0 <= i - s < tiles_of(last):
+                add_back(last, s, i - s)
+    for c, s in left:
+        if s == bits - 1:
+            add_all(c, s)
 
     for c in range(len(chunks)):
         for k in range(1, group):
             amp_copy(c, k).wait_send()
         for s in range(bits):
-            for t in range(tiles):
+            for t in range(tiles_of(c)):
                 back_copy(c, s, t).wait_send()
 
 
@@ -177,7 +201,7 @@
     count = amplitudes.shape[0]
     depth, columns = integrals.shape
     bits = group.bit_length() - 1
-    tiles = columns // TILE
+    tiles = columns // min(RETURN, LAST)
     chunks = CHUNKS
     most = group * max(chunks)
     n = len(chunks)

time: 120 us -> 108 us (0.900)
  Pallas kernels: 116 us -> 104 us
    pallas_call x1, Pallas kernels: 116 us -> 104 us  [body(): pl.pallas_call(functools.partial(kernel, group, layers, chunks), out_shap...]
where the time goes in v2:
time: 108 us
  Pallas kernels  104 us (96%)
  other arithmetic  2.74 us (3%)
    pallas_call x1, Pallas kernels, body(): pl.pallas_call(functools.partial(kernel, group, layers, chunks), out_shap...  104 us

profile of v2, /device:TPU:0, one launch (start us, length us, event | category | flops | bytes accessed | tf_op | source)
XLA Modules:
  0.0 107.9 jit_solution(6983378332266015856)
XLA Ops:
  0.0 0.8 slice_bitcast_fusion
  0.8 0.9 select_reduce_fusion.1
  1.6 0.0 copy-start
  1.6 104.3 %shard_map.55 = f32[48,2048]{1,0:T(8,128)} custom-call(f32[48,16384]{1,0:T(8,128)} %amp.1, f32[2048,2048]{1,0:T(8,128)} %ints.1), custom_call_target="tpu_custom_call" | custom-call | flops 9663676416 | bytes 19922944 | tf_op jit(solution)/shard_map/pallas_call | solution.py:208
  106.0 0.0 copy-done
  106.0 1.9 %subtract_divide_fusion = f32[48,2048]{1,0:T(8,128)} fusion(f32[48,2048]{1,0:T(8,128)} %shard_map.55, f32[48]{0:T(128)S(1)} %get-tuple-element.6, f32[48]{0:T(128)S(1)} %get-tuple-element.5, f32[2048]{0:T(1024)S(1)} %copy-done), kind=kLoop, calls=%fused_computation | loop fusion | flops 294912 | bytes 795008 | tf_op jit(solution)/shard_map/div | solution.py:239
Async XLA Ops:
  1.6 104.3 %copy-start = (f32[2048]{0:T(1024)S(1)}, f32[2048]{0:T(1024)}, u32[]{:S(2)}) copy-start(f32[2048]{0:T(1024)} %param.9) | copy-start | bytes 24580
